TPU v7x, 32 devices: a whole 2x2x4 slice. The times are simulated.
32 devices in a mesh: ex: 4 (over y, core), proj: 8 (over z, x).
Axes of the slice: x: 2, y: 2, z: 4, core: 2. Of those that a mesh axis runs over, the one named last changes fastest.
Arguments:
- queries: bfloat16 [1024, 65536], P('ex', 'proj'), as said below
- train_grads: bfloat16 [2048, 65536], P('ex', 'proj'), as said below
- query_weight: float32 [1024], P('proj'), may hold values from 0.3 to 3
Outputs:
- scores: bfloat16 [1024, 2048], P('proj', 'ex')
- influence: float32 [2048], P('ex')
Inputs may be any that keep to these rules, and one draw needn't show every extreme that they name: `queries`: finite real gradient entries. `train_grads`: finite real gradient entries.
All inputs are finite; a program needn't handle non-finite values.
Results may differ from a plain program's by a relative error of at most 0.00055.
Values may be sent and summed in bfloat16 or wider, within the bound.
A program may use at most 128 MiB of HBM per device.

v0:
```python
import jax
import jax.numpy as jnp
from jax import lax
from jax.sharding import PartitionSpec as P

P_SIZE = 8192
LAYERS = 8
NQ = 1024


def body(queries, train_grads, query_weight):
    own_rows = query_weight.shape[0]
    partial_value = lax.dot_general(
        lax.all_gather(queries, "ex", axis=0, tiled=True),
        train_grads,
        (((1,), (1,)), ((), ())),
        preferred_element_type=jnp.float32,
    )
    local_q = queries.astype(jnp.float32)
    query_part = lax.all_gather(jnp.sum(local_q * local_q, axis=1), "ex", axis=0, tiled=True)
    local_t = train_grads.astype(jnp.float32)
    train_part = jnp.sum(local_t * local_t, axis=1)
    query_total, train_sq = lax.psum((query_part, train_part), "proj")
    dots = lax.psum_scatter(partial_value, "proj", scatter_dimension=0, tiled=True)
    offset = lax.axis_index("proj") * own_rows
    query_sq = lax.dynamic_slice_in_dim(query_total, offset, own_rows, 0)
    scaled = (
        (LAYERS * P_SIZE) ** 0.5
        * dots
        * lax.rsqrt(query_sq + 1e-06)[:, None]
        * lax.rsqrt(train_sq + 1e-06)[None, :]
    )
    scores = scaled.astype(jnp.bfloat16)
    weighted = jnp.dot(query_weight, scaled, precision=lax.Precision.HIGHEST)
    influence = lax.psum(weighted, "proj") * NQ ** (-0.5)
    return (scores, influence)


def solution(mesh):
    return jax.shard_map(
        body,
        mesh=mesh,
        in_specs=(P("ex", "proj"), P("ex", "proj"), P("proj")),
        out_specs=(P("proj", "ex"), P("ex")),
        check_vma=False,
    )
```

profile of v0, /device:TPU:0, one launch (start us, length us, event | category | flops | bytes accessed | tf_op | source)
XLA Modules:
  0.0 232.3 jit_solution(12687964593389319212)
XLA Ops:
  7.2 0.0 copy-start
  7.2 0.0 all-gather.3.cloned.1.call-start
  7.2 0.7 all-gather.3.cloned.1.call-update
  7.9 0.0 reduce-scatter.2.cloned.1.call-start
  8.0 110.3 %all-gather.3.cloned.1.call-done = bf16[1024,8192]{1,0:T(8,128)(2,1)} async-done(((bf16[256,8192]{1,0:T(8,128)(2,1)}), bf16[1024,8192]{1,0:T(8,128)(2,1)}) %all-gather.3.cloned.1.call-update) | async-done | bytes 16777232 | tf_op jit(solution)/shard_map/all_gather | solution.py:14
  118.2 15.9 %fusion.5 = f32[1024,512]{1,0:T(8,128)} fusion(bf16[1024,8192]{1,0:T(8,128)(2,1)} %all-gather.3.cloned.1.call-done, bf16[512,8192]{1,0:T(8,128)(2,1)} %param.4), kind=kOutput, calls=%fused_computation.11 | convolution fusion | flops 8589934592 | bytes 27262976 | tf_op jit(solution)/shard_map/dot_general | solution.py:13
  134.1 0.0 reduce-scatter.2.cloned.1.call-update
  134.1 3.1 %multiply_reduce_fusion.1 = f32[256]{0:T(256)S(1)} fusion(bf16[256,8192]{1,0:T(8,128)(2,1)} %param.3), kind=kLoop, calls=%fused_computation.1 | loop fusion | flops 6291200 | bytes 4195328 | tf_op jit(solution)/shard_map/reduce_sum | solution.py:20
  137.2 5.1 %all-gather = f32[4,1,256]{2,1,0:T(1,128)S(1)} all-gather(f32[1,1,256]{2,1,0:T(1,128)S(1)} %bitcast.10), channel_id=1, replica_groups=mesh['ex'=4,'proj'=8] {'ex'}, dimensions={0}, use_global_device_ids=true | all-gather | bytes 5120 | tf_op jit(solution)/shard_map/all_gather | solution.py:20
  142.3 5.1 %multiply_reduce_fusion = f32[512]{0:T(512)S(1)} fusion(bf16[512,8192]{1,0:T(8,128)(2,1)} %param.4), kind=kLoop, calls=%fused_computation | loop fusion | flops 12582400 | bytes 8390656 | tf_op jit(solution)/shard_map/reduce_sum | solution.py:22
  147.4 21.8 %all-reduce = (f32[512]{0:T(512)S(1)}, f32[1024]{0:T(1024)S(1)}) all-reduce(f32[512]{0:T(512)S(1)} %multiply_reduce_fusion, f32[1024]{0:T(1024)S(1)} %bitcast.8), channel_id=1, replica_groups=mesh['ex'=4,'proj'=8] {'proj'}, use_global_device_ids=true, to_apply=%region_4.0 | all-reduce | flops 1536 | bytes 12288 | tf_op jit(solution)/shard_map/psum | solution.py:23
  169.2 0.1 rsqrt_multiply_fusion
  169.3 33.4 %reduce-scatter.2.cloned.1.call-done = f32[128,512]{1,0:T(8,128)} async-done(((f32[1024,512]{1,0:T(8,128)}), f32[128,512]{1,0:T(8,128)}) %reduce-scatter.2.cloned.1.call-update) | async-done | bytes 262160 | tf_op jit(solution)/shard_map/reduce_scatter | solution.py:24
  202.7 0.0 copy-done
  202.7 1.3 fusion
  204.0 19.1 %psum.23 = f32[512]{0:T(512)S(1)} all-reduce(f32[512]{0:T(512)S(1)} %bitcast.9), channel_id=1, replica_groups=mesh['ex'=4,'proj'=8] {'proj'}, use_global_device_ids=true, to_apply=%region_5.0 | all-reduce | flops 512 | bytes 4096 | tf_op jit(solution)/shard_map/psum | solution.py:35
  223.1 0.6 broadcast_multiply_fusion
  223.7 1.7 fusion.1
  (1 shorter events, 0.0 us)
Async XLA Ops:
  7.2 195.6 %copy-start = (f32[128]{0:T(128)S(1)}, f32[128]{0:T(128)}, u32[]{:S(2)}) copy-start(f32[128]{0:T(128)} %param.5) | copy-start | bytes 1540
  7.2 111.1 %all-gather.3.cloned.1.call-start = ((), (), s32[]{:S(2)}) async-start(), calls=%async_computation.1 | async-start | bytes 20971520 | tf_op jit(solution)/shard_map/all_gather | solution.py:14
  7.9 194.8 %reduce-scatter.2.cloned.1.call-start = ((), (), s32[]{:S(2)}) async-start(), calls=%async_computation.2 | async-start | bytes 2359296 | tf_op jit(solution)/shard_map/reduce_scatter | solution.py:24
Sparse Core Ops, SparseCore 0:
  9.6 108.6 all-gather.2
  134.2 68.4 reduce-scatter.1
where the time goes:
time: 233 us; the launch traced here: 232 us
  waiting for transfers between devices  144 us (62%)
  blocking collectives  46 us (20%)
  matrix products  17.1 us (7%)
  between operations  14.1 us (6%)
  other arithmetic  10.6 us (5%)
    all_gather x1, waiting for transfers between devices, body(): lax.all_gather(queries, 'ex', axis=0, tiled=True)  110 us
    reduce_scatter x1, waiting for transfers between devices, body(): lax.psum_scatter(partial_value, 'proj', scatter_dimension=0, tiled=True)  33.4 us
    psum x1, blocking collectives, body(): query_total, train_sq = lax.psum((query_part, train_part), 'proj')  21.8 us
    psum x1, blocking collectives, body(): influence = lax.psum(weighted, 'proj') * NQ ** (-0.5)  19.1 us
    dot_general x1, matrix products, body(): lax.dot_general(lax.all_gather(queries, 'ex', axis=0, tiled=True), train_...  15.9 us
    reduce_sum x1, other arithmetic, body(): train_part = jnp.sum(local_t * local_t, axis=1)  5.1 us
    all_gather x1, blocking collectives, body(): lax.all_gather(jnp.sum(local_q * local_q, axis=1), 'ex', axis=0, tiled=True)  5.06 us
  transfers between devices with their start and end apart: 2, of which 2 were waited for; matrix products, arithmetic and copies ran while one was open for 4% of the time, Pallas kernels for 0%

commit v1 on v0

v1 whole, which is shorter than its diff:
```python
import functools

import jax
import jax.numpy as jnp
from jax import lax
from jax.experimental import pallas as pl
from jax.experimental.pallas import tpu as pltpu
from jax.sharding import PartitionSpec as P

MESH = pl.DeviceIdType.MESH
SLAB = 16
AHEAD = 2
LANES = 128


def kernel(
    ex, proj, q_hbm, t_hbm, w_ref,
    scores_ref, infl_ref,
    qbuf, tbuf, part, rs_buf, tacc, t_own, t_buf, i_own, i_buf, scaled_ref,
    load_sem, y_send, y_recv, sib_send, sib_recv, rs_send, rs_recv, t_send, t_recv, i_send, i_recv,
):
    nb, rows_p, cols = q_hbm.shape
    n = t_hbm.shape[0]
    chips = ex // 2
    chunks = rows_p // SLAB
    group = 2 * nb
    e = lax.axis_index("ex")
    p = lax.axis_index("proj")
    y, core = e // 2, e % 2
    sibling = e + 1 - 2 * core

    load_t = pltpu.make_async_copy(t_hbm, tbuf, load_sem.at[0])
    load_q = pltpu.make_async_copy(q_hbm, qbuf.at[pl.ds(e * nb, nb)], load_sem.at[1])

    barrier = pltpu.get_barrier_semaphore()
    for d in range(1, chips):
        pl.semaphore_signal(barrier, inc=1, device_id={"ex": lax.rem(y + d, chips) * 2 + core}, device_id_type=MESH)
    pl.semaphore_signal(barrier, inc=1, device_id={"ex": sibling}, device_id_type=MESH)
    for d in range(1, proj):
        pl.semaphore_signal(barrier, inc=1, device_id={"proj": lax.rem(p + d, proj)}, device_id_type=MESH)
    load_t.start()
    load_q.start()
    pl.semaphore_wait(barrier, chips + proj - 1)

    def rows_of(c):
        return pl.ds(pl.multiple_of(c * SLAB, SLAB), SLAB)

    def send_y(i):
        d, c = i // chunks, lax.rem(i, chunks)
        pltpu.make_async_remote_copy(
            src_ref=q_hbm.at[:, rows_of(c)],
            dst_ref=qbuf.at[pl.ds(e * nb, nb), rows_of(c)],
            send_sem=y_send.at[d],
            recv_sem=y_recv.at[d, c],
            device_id={"ex": lax.rem(y + d + 1, chips) * 2 + core},
            device_id_type=MESH,
        ).start()

    def sib_copy(s, c, own):
        at = (lax.rem(y - s + chips, chips) * 2 + core) * nb
        dst = qbuf.at[pl.ds(at, nb), rows_of(c)]
        return pltpu.make_async_remote_copy(
            src_ref=q_hbm.at[:, rows_of(c)] if own else dst,
            dst_ref=dst,
            send_sem=sib_send.at[s],
            recv_sem=sib_recv.at[s, c],
            device_id={"ex": sibling},
            device_id_type=MESH,
        )

    total = (chips - 1) * chunks
    for i in range(min(AHEAD, total)):
        send_y(jnp.int32(i))
    for c in range(chunks):
        sib_copy(0, c, True).start()

    load_t.wait()

    def t_rows(g, carry):
        rows = pl.ds(pl.multiple_of(g * SLAB, SLAB), SLAB)
        acc = jnp.zeros((SLAB, LANES), jnp.float32)
        for k in range(0, cols, LANES):
            x = tbuf[rows, k : k + LANES].astype(jnp.float32)
            acc = acc + x * x
        tacc[rows, :] = acc
        return carry

    lax.fori_loop(0, n // SLAB, t_rows, 0)
    t_own[...] = jnp.sum(tacc[...].T.reshape(LANES // 8, 8, n), axis=0)

    def to_all(src, buf, send, recv):
        for d in range(1, proj):
            pltpu.make_async_remote_copy(
                src_ref=src,
                dst_ref=buf.at[d - 1],
                send_sem=send.at[0],
                recv_sem=recv.at[0],
                device_id={"proj": lax.rem(p + d, proj)},
                device_id_type=MESH,
            ).start()

    def wait_for(ref, sem):
        pltpu.make_async_copy(ref, ref, sem).wait()

    to_all(t_own, t_buf, t_send, t_recv)
    load_q.wait()

    def finish(c):
        rows = rows_of(c)
        wait_for(rs_buf.at[:, rows], rs_recv.at[c])
        tot = part[p, rows, :]
        for j in range(proj - 1):
            tot = tot + rs_buf[j, rows, :]
        query_sq = jnp.sum(tot[:, n:], axis=1, keepdims=True)
        scaled = (
            float(cols * proj) ** 0.5
            * tot[:, :n]
            * lax.rsqrt(query_sq + 1e-06)
            * lax.rsqrt(t_own[0:1, :] + 1e-06)
        )
        scaled_ref[rows, :] = scaled
        scores_ref[rows, :] = scaled.astype(jnp.bfloat16)

    def step(i, carry):
        s, c = i // chunks, lax.rem(i, chunks)
        late = i - chunks
        chip = lax.rem(y - s + chips, chips)

        @pl.when(s > 0)
        def _():
            got = qbuf.at[pl.ds((chip * 2 + core) * nb, nb), rows_of(c)]
            wait_for(got, y_recv.at[s - 1, c])
            sib_copy(s, c, False).start()

            @pl.when(late + AHEAD < total)
            def _():
                send_y(late + AHEAD)

        wait_for(qbuf.at[pl.ds((chip * 2 + 1 - core) * nb, nb), rows_of(c)], sib_recv.at[s, c])
        blocks = pl.ds(chip * group, group)
        depth = min(cols, 2048)
        acc = jnp.zeros((group * SLAB, n), jnp.float32)
        for k in range(0, cols, depth):
            x = qbuf[blocks, rows_of(c), k : k + depth].reshape(group * SLAB, depth)
            acc = acc + lax.dot_general(
                x, tbuf[:, k : k + depth], (((1,), (1,)), ((), ())), preferred_element_type=jnp.float32
            )
        part[blocks, rows_of(c), :n] = acc.reshape(group, SLAB, n)
        sq = jnp.zeros((group, SLAB, LANES), jnp.float32)
        for k in range(0, cols, LANES):
            x = qbuf[blocks, rows_of(c), k : k + LANES].astype(jnp.float32)
            sq = sq + x * x
        part[blocks, rows_of(c), n:] = sq
        for b in range(group):
            to = chip * group + b

            @pl.when(to != p)
            def _():
                pltpu.make_async_remote_copy(
                    src_ref=part.at[to, rows_of(c)],
                    dst_ref=rs_buf.at[lax.rem(to - p + proj, proj) - 1, rows_of(c)],
                    send_sem=rs_send.at[0],
                    recv_sem=rs_recv.at[c],
                    device_id={"proj": to},
                    device_id_type=MESH,
                ).start()

        @pl.when(i == chunks * chips - chunks)
        def _():
            wait_for(t_buf, t_send.at[0])
            wait_for(t_buf, t_recv.at[0])
            tot = t_own[...]
            for j in range(proj - 1):
                tot = tot + t_buf[j]
            t_own[...] = jnp.broadcast_to(jnp.sum(tot, axis=0, keepdims=True), tot.shape)

        @pl.when(i > chunks * chips - chunks)
        def _():
            finish(c - 1)

        return carry

    lax.fori_loop(0, chips * chunks, step, 0)
    finish(jnp.int32(chunks - 1))

    weighted = jnp.dot(
        jnp.broadcast_to(w_ref[...], (8, rows_p)),
        scaled_ref[...],
        precision=lax.Precision.HIGHEST,
        preferred_element_type=jnp.float32,
    )
    i_own[...] = weighted
    to_all(i_own, i_buf, i_send, i_recv)
    for s in range(chips):
        wait_for(q_hbm, sib_send.at[s])
    for d in range(chips - 1):
        wait_for(q_hbm, y_send.at[d])
    wait_for(rs_buf, rs_send.at[0])
    wait_for(i_buf, i_recv.at[0])
    tot = weighted
    for j in range(proj - 1):
        tot = tot + i_buf[j]
    infl_ref[...] = tot[0:1, :] * (proj * rows_p) ** (-0.5)
    wait_for(i_buf, i_send.at[0])


def body(ex, proj, queries, train_grads, query_weight):
    rows, cols = queries.shape
    n = train_grads.shape[0]
    rows_p = query_weight.shape[0]
    nb = rows // rows_p
    chips, chunks = ex // 2, rows_p // SLAB
    width = n + LANES
    f32, bf16 = jnp.float32, jnp.bfloat16
    vmem = pl.BlockSpec(memory_space=pltpu.VMEM)
    anywhere = pl.BlockSpec(memory_space=pl.ANY)
    dma = pltpu.SemaphoreType.DMA
    scores, influence = pl.pallas_call(
        functools.partial(kernel, ex, proj),
        out_shape=(jax.ShapeDtypeStruct((rows_p, n), bf16), jax.ShapeDtypeStruct((1, n), f32)),
        in_specs=[anywhere, anywhere, vmem],
        out_specs=(vmem, vmem),
        scratch_shapes=[
            pltpu.VMEM((proj, rows_p, cols), bf16),
            pltpu.VMEM((n, cols), bf16),
            pltpu.VMEM((proj, rows_p, width), f32),
            pltpu.VMEM((proj - 1, rows_p, width), f32),
            pltpu.VMEM((n, LANES), f32),
            pltpu.VMEM((8, n), f32),
            pltpu.VMEM((proj - 1, 8, n), f32),
            pltpu.VMEM((8, n), f32),
            pltpu.VMEM((proj - 1, 8, n), f32),
            pltpu.VMEM((rows_p, n), f32),
            dma((2,)),
            dma((chips - 1,)),
            dma((chips - 1, chunks)),
            dma((chips,)),
            dma((chips, chunks)),
            dma((1,)),
            dma((chunks,)),
            dma((1,)),
            dma((1,)),
            dma((1,)),
            dma((1,)),
        ],
        compiler_params=pltpu.CompilerParams(
            collective_id=0, has_side_effects=True, vmem_limit_bytes=56 * 2**20
        ),
        name="scores_ring",
    )(queries.reshape(nb, rows_p, cols), train_grads, query_weight.reshape(1, rows_p))
    return scores, influence.reshape(n)


def solution(mesh):
    return jax.shard_map(
        functools.partial(body, mesh.shape["ex"], mesh.shape["proj"]),
        mesh=mesh,
        in_specs=(P("ex", "proj"), P("ex", "proj"), P("proj")),
        out_specs=(P("proj", "ex"), P("ex")),
        check_vma=False,
    )
```

time: 233 us -> 126 us (0.54)
  waiting for transfers between devices: 144 us -> 0 us
  Pallas kernels: 0 us -> 122 us
  blocking collectives: 46 us -> 0 us
  matrix products: 17.1 us -> 0 us
  between operations: 14.1 us -> 0.64 us
  other arithmetic: 10.6 us -> 0 us
  local copies, waits for them, and re-layouts: 0.01 us -> 2.83 us
    pallas_call x0 -> x1, Pallas kernels: none -> 122 us  [body(): pl.pallas_call(functools.partial(kernel, ex, proj), out_shape=(jax.ShapeD...]
    all_gather x1 -> x0, waiting for transfers between devices: 110 us -> none  [body(): lax.all_gather(queries, 'ex', axis=0, tiled=True)]
    psum x2 -> x0, blocking collectives: 40.9 us -> none  [the longest x1 21.8 us: body(): query_total, train_sq = lax.psum((query_part, train_part), 'proj')]
    reduce_scatter x1 -> x0, waiting for transfers between devices: 33.4 us -> none  [body(): lax.psum_scatter(partial_value, 'proj', scatter_dimension=0, tiled=True)]
    dot_general x2 -> x0, matrix products: 17.1 us -> none  [the longest x1 15.9 us: body(): lax.dot_general(lax.all_gather(queries, 'ex', axis=0, tiled=True), train_...]
    reduce_sum x2 -> x0, other arithmetic: 8.21 us -> none  [the longest x1 5.1 us: body(): train_part = jnp.sum(local_t * local_t, axis=1)]
    all_gather x1 -> x0, blocking collectives: 5.06 us -> none  [body(): lax.all_gather(jnp.sum(local_q * local_q, axis=1), 'ex', axis=0, tiled=True)]
    unnamed x2, local copies, waits for them, and re-layouts: 0.01 us -> 2.83 us
  transfers between devices with their start and end apart: 2 -> 0, of which waited for: 2 -> 0; matrix products, arithmetic and copies ran while one was open for 4% -> 0% of each run, Pallas kernels for 0% -> 0%
where the time goes in v1:
time: 126 us
  Pallas kernels  122 us (97%)
  local copies, waits for them, and re-layouts  2.83 us (2%)
    pallas_call x1, Pallas kernels, body(): pl.pallas_call(functools.partial(kernel, ex, proj), out_shape=(jax.ShapeD...  122 us
    unnamed x2, local copies, waits for them, and re-layouts  2.83 us

profile of v1, /device:TPU:0, one launch (start us, length us, event | category | flops | bytes accessed | tf_op | source)
XLA Modules:
  0.0 125.7 jit_solution(17487078637365337443)
XLA Ops:
  0.6 122.3 %scores_ring.1 = (bf16[128,512]{1,0:T(8,128)(2,1)}, f32[1,512]{1,0:T(1,128)}) custom-call(bf16[2,128,8192]{2,1,0:T(8,128)(2,1)} %bitcast.3, bf16[512,8192]{1,0:T(8,128)(2,1)} %t_hbm.1, f32[1,128]{1,0:T(1,128)} %bitcast.5), custom_call_target="tpu_custom_call" | custom-call | tf_op jit(solution)/shard_map/scores_ring/pallas_call | solution.py:218
  122.9 1.6 %copy.7 = bf16[128,512]{1,0:T(8,128)(2,1)} copy(bf16[128,512]{1,0:T(8,128)(2,1)} %get-tuple-element.8) | data formatting | bytes 262144
  124.5 1.3 %copy.8 = f32[512]{0:T(512)} copy(f32[512]{0:T(512)} %bitcast.4) | data formatting | bytes 4096

commit v2 on v1

v2 whole, which is shorter than its diff:
```python
import functools

import jax
import jax.numpy as jnp
from jax import lax
from jax.experimental import pallas as pl
from jax.experimental.pallas import tpu as pltpu
from jax.sharding import PartitionSpec as P

MESH = pl.DeviceIdType.MESH
SLAB = 16
FIRST = 2
LANES = 128
PROMPT = 3


def kernel(
    ex, proj, q_hbm, t_hbm, w_ref,
    scores_ref, infl_ref,
    qbuf, tbuf, part, pair_buf, rs_buf, lanes, m_own, m_buf, w_buf, q_rows, q_col, wq_col, t_scale, v_own, v_buf,
    load_sem, y_send, y_recv, sib_send, sib_recv, pair_send, pair_recv, rs_send, rs_recv,
    m_send, m_recv, w_send, w_recv, n_send, n_recv, v_send, v_recv,
):
    nb, rows_p, cols = q_hbm.shape
    n = t_hbm.shape[0]
    rows_e = nb * rows_p
    chips = ex // 2
    half = proj // 2
    chunks = rows_p // SLAB
    group = 2 * nb
    e = lax.axis_index("ex")
    p = lax.axis_index("proj")
    y, core = e // 2, e % 2
    z, x = p // 2, p % 2
    sibling = e + 1 - 2 * core
    partner = p + 1 - 2 * x

    load_t = pltpu.make_async_copy(t_hbm, tbuf, load_sem.at[0])
    load_q = pltpu.make_async_copy(q_hbm, qbuf.at[pl.ds(e * nb, nb)], load_sem.at[1])

    barrier = pltpu.get_barrier_semaphore()
    for d in range(1, ex):
        pl.semaphore_signal(barrier, inc=1, device_id={"ex": lax.rem(e + d, ex)}, device_id_type=MESH)
    for d in range(1, proj):
        pl.semaphore_signal(barrier, inc=1, device_id={"proj": lax.rem(p + d, proj)}, device_id_type=MESH)
    load_q.start()
    load_t.start()
    pl.semaphore_wait(barrier, ex + proj - 2)

    def rows_of(c):
        return pl.ds(pl.multiple_of(c * SLAB, SLAB), SLAB)

    def send_y(i):
        d, c = i // chunks, lax.rem(i, chunks)
        pltpu.make_async_remote_copy(
            src_ref=q_hbm.at[:, rows_of(c)],
            dst_ref=qbuf.at[pl.ds(e * nb, nb), rows_of(c)],
            send_sem=y_send.at[d],
            recv_sem=y_recv.at[d, c],
            device_id={"ex": lax.rem(y + d + 1, chips) * 2 + core},
            device_id_type=MESH,
        ).start()

    def sib_copy(s, c, own):
        at = (lax.rem(y - s + chips, chips) * 2 + core) * nb
        dst = qbuf.at[pl.ds(at, nb), rows_of(c)]
        return pltpu.make_async_remote_copy(
            src_ref=q_hbm.at[:, rows_of(c)] if own else dst,
            dst_ref=dst,
            send_sem=sib_send.at[s],
            recv_sem=sib_recv.at[s, c],
            device_id={"ex": sibling},
            device_id_type=MESH,
        )

    total = (chips - 1) * chunks
    for i in range(min(FIRST, total)):
        send_y(jnp.int32(i))

    def to_all(src, slot, send, recv):
        for d in range(1, proj):
            pltpu.make_async_remote_copy(
                src_ref=src,
                dst_ref=slot(d),
                send_sem=send.at[0],
                recv_sem=recv.at[0],
                device_id={"proj": lax.rem(p + d, proj)},
                device_id_type=MESH,
            ).start()

    def wait_for(ref, sem):
        pltpu.make_async_copy(ref, ref, sem).wait()

    w_buf[0] = jnp.broadcast_to(w_ref[...], (8, rows_p))
    to_all(w_buf.at[0], lambda d: w_buf.at[d], w_send, w_recv)
    for c in range(chunks):
        sib_copy(0, c, True).start()

    def norms(count, at, load):
        def one(g, carry):
            acc = jnp.zeros((SLAB, LANES), jnp.float32)
            for k in range(0, cols, LANES):
                v = load(g, k).astype(jnp.float32)
                acc = acc + v * v
            lanes[pl.ds(pl.multiple_of(at + g * SLAB, SLAB), SLAB), :] = acc
            return carry

        lax.fori_loop(0, count // SLAB, one, 0)

    load_q.wait()
    norms(rows_e, n, lambda g, k: qbuf[e * nb + g // chunks, rows_of(lax.rem(g, chunks)), k : k + LANES])
    load_t.wait()
    norms(n, 0, lambda g, k: tbuf[rows_of(g), k : k + LANES])
    m_own[...] = jnp.sum(lanes[...].T.reshape(LANES // 8, 8, n + rows_e), axis=0)
    to_all(m_own, lambda d: m_buf.at[d - 1], m_send, m_recv)
    wait_for(m_buf, m_recv.at[0])
    tot = m_own[...]
    for j in range(proj - 1):
        tot = tot + m_buf[j]
    tot = jnp.broadcast_to(jnp.sum(tot, axis=0, keepdims=True), tot.shape)
    scale = lax.rsqrt(tot + 1e-06)
    t_scale[...] = scale[:, :n]
    q_rows[0] = scale[:, n:]
    for d in range(1, ex):
        pltpu.make_async_remote_copy(
            src_ref=q_rows.at[0],
            dst_ref=q_rows.at[d],
            send_sem=n_send.at[0],
            recv_sem=n_recv.at[jnp.where(lax.rem(e + d, ex) == sibling, 0, 1)],
            device_id={"ex": lax.rem(e + d, ex)},
            device_id_type=MESH,
        ).start()
    for i in range(min(FIRST, total), total):
        send_y(jnp.int32(i))
    wait_for(w_buf.at[pl.ds(1, proj - 1)], w_recv.at[0])
    for d in range(proj):
        row = jnp.broadcast_to(w_buf[d, 0:1, :], (LANES, rows_p))
        wq_col[lax.rem(p - d + proj, proj)] = row.T

    def columns(source):
        blocks = pl.ds(source * nb, nb)
        row = q_rows[lax.rem(e - source + ex, ex), 0:1, :]
        col = jnp.broadcast_to(row, (LANES, rows_e)).T.reshape(nb, rows_p, LANES)
        q_col[blocks] = col
        wq_col[blocks] = wq_col[blocks] * col

    columns(e)
    wait_for(q_rows.at[pl.ds(1, 1)], n_recv.at[0])
    columns(sibling)
    v_own[...] = jnp.zeros_like(v_own)

    def finish(c):
        rows = rows_of(c)
        wait_for(rs_buf.at[:, rows], rs_recv.at[c])
        tot = part[z, x, rows, :]
        for j in range(half - 1):
            tot = tot + rs_buf[j, rows, :]
        scaled = float(cols * proj) ** 0.5 * tot * q_col[p, rows, 0:1] * t_scale[0:1, :]
        scores_ref[rows, :] = scaled.astype(jnp.bfloat16)

    def pass_on(i):
        s, c = i // chunks, lax.rem(i, chunks)
        chip = lax.rem(y - s + chips, chips)
        pairs = pl.ds(chip * nb, nb)
        wait_for(pair_buf.at[pairs, rows_of(c)], pair_recv.at[s, c])
        part[pairs, x, rows_of(c), :] = part[pairs, x, rows_of(c), :] + pair_buf[pairs, rows_of(c), :]
        for b in range(nb):
            to = chip * nb + b

            @pl.when(to != z)
            def _():
                pltpu.make_async_remote_copy(
                    src_ref=part.at[to, x, rows_of(c)],
                    dst_ref=rs_buf.at[lax.rem(to - z + half, half) - 1, rows_of(c)],
                    send_sem=rs_send.at[0],
                    recv_sem=rs_recv.at[c],
                    device_id={"proj": 2 * to + x},
                    device_id_type=MESH,
                ).start()

    prompt = chips * chunks - min(chunks, PROMPT)

    def step(i, carry):
        s, c = i // chunks, lax.rem(i, chunks)
        chip = lax.rem(y - s + chips, chips)

        @pl.when(i == chunks)
        def _():
            wait_for(q_rows.at[pl.ds(1, ex - 2)], n_recv.at[1])
            for d in range(1, chips):
                for k in range(2):
                    columns(lax.rem(y + d, chips) * 2 + k)

        @pl.when(s > 0)
        def _():
            got = qbuf.at[pl.ds((chip * 2 + core) * nb, nb), rows_of(c)]
            wait_for(got, y_recv.at[s - 1, c])
            sib_copy(s, c, False).start()

        wait_for(qbuf.at[pl.ds((chip * 2 + 1 - core) * nb, nb), rows_of(c)], sib_recv.at[s, c])
        blocks = pl.ds(chip * group, group)
        pairs = pl.ds(chip * nb, nb)
        depth = min(cols, 2048)
        acc = jnp.zeros((group * SLAB, n), jnp.float32)
        for k in range(0, cols, depth):
            q = qbuf[blocks, rows_of(c), k : k + depth].reshape(group * SLAB, depth)
            acc = acc + lax.dot_general(
                q, tbuf[:, k : k + depth], (((1,), (1,)), ((), ())), preferred_element_type=jnp.float32
            )
        part[pairs, :, rows_of(c), :] = acc.reshape(nb, 2, SLAB, n)
        pltpu.make_async_remote_copy(
            src_ref=part.at[pairs, 1 - x, rows_of(c)],
            dst_ref=pair_buf.at[pairs, rows_of(c)],
            send_sem=pair_send.at[s],
            recv_sem=pair_recv.at[s, c],
            device_id={"proj": partner},
            device_id_type=MESH,
        ).start()
        weighted = acc * wq_col[blocks, rows_of(c), 0:1].reshape(group * SLAB, 1)
        v_own[...] = v_own[...] + jnp.sum(weighted.reshape(group * SLAB // 8, 8, n), axis=0)

        @pl.when(i == chips * chunks - 1)
        def _():
            to_all(v_own, lambda d: v_buf.at[d - 1], v_send, v_recv)

        @pl.when((i > 0) & (i <= prompt))
        def _():
            pass_on(i - 1)

        @pl.when(i >= prompt)
        def _():
            pass_on(i)

        @pl.when(i > chunks * chips - chunks + 1)
        def _():
            finish(c - 2)

        return carry

    lax.fori_loop(0, chips * chunks, step, 0)
    wait_for(v_buf, v_recv.at[0])
    tot = v_own[...]
    for j in range(proj - 1):
        tot = tot + v_buf[j]
    tot = jnp.sum(tot, axis=0, keepdims=True) * t_scale[0:1, :]
    infl_ref[...] = tot * (float(cols * proj) ** 0.5 * (proj * rows_p) ** (-0.5))
    for c in range(max(chunks - 2, 0), chunks):
        finish(jnp.int32(c))

    for s in range(chips):
        wait_for(q_hbm, sib_send.at[s])
        wait_for(pair_buf.at[pl.ds(0, nb)], pair_send.at[s])
    for d in range(chips - 1):
        wait_for(q_hbm, y_send.at[d])
    wait_for(rs_buf, rs_send.at[0])
    wait_for(m_buf, m_send.at[0])
    wait_for(w_buf.at[pl.ds(1, proj - 1)], w_send.at[0])
    wait_for(q_rows.at[pl.ds(1, ex - 1)], n_send.at[0])
    wait_for(v_buf, v_send.at[0])


def body(ex, proj, queries, train_grads, query_weight):
    rows, cols = queries.shape
    n = train_grads.shape[0]
    rows_p = query_weight.shape[0]
    nb = rows // rows_p
    chips, chunks = ex // 2, rows_p // SLAB
    half = proj // 2
    f32, bf16 = jnp.float32, jnp.bfloat16
    vmem = pl.BlockSpec(memory_space=pltpu.VMEM)
    anywhere = pl.BlockSpec(memory_space=pl.ANY)
    dma = pltpu.SemaphoreType.DMA
    scores, influence = pl.pallas_call(
        functools.partial(kernel, ex, proj),
        out_shape=(jax.ShapeDtypeStruct((rows_p, n), bf16), jax.ShapeDtypeStruct((1, n), f32)),
        in_specs=[anywhere, anywhere, vmem],
        out_specs=(vmem, vmem),
        scratch_shapes=[
            pltpu.VMEM((proj, rows_p, cols), bf16),
            pltpu.VMEM((n, cols), bf16),
            pltpu.VMEM((half, 2, rows_p, n), f32),
            pltpu.VMEM((half, rows_p, n), f32),
            pltpu.VMEM((half - 1, rows_p, n), f32),
            pltpu.VMEM((n + rows, LANES), f32),
            pltpu.VMEM((8, n + rows), f32),
            pltpu.VMEM((proj - 1, 8, n + rows), f32),
            pltpu.VMEM((proj, 8, rows_p), f32),
            pltpu.VMEM((ex, 8, rows), f32),
            pltpu.VMEM((proj, rows_p, LANES), f32),
            pltpu.VMEM((proj, rows_p, LANES), f32),
            pltpu.VMEM((8, n), f32),
            pltpu.VMEM((8, n), f32),
            pltpu.VMEM((proj - 1, 8, n), f32),
            dma((2,)),
            dma((chips - 1,)),
            dma((chips - 1, chunks)),
            dma((chips,)),
            dma((chips, chunks)),
            dma((chips,)),
            dma((chips, chunks)),
            dma((1,)),
            dma((chunks,)),
            dma((1,)),
            dma((1,)),
            dma((1,)),
            dma((1,)),
            dma((1,)),
            dma((2,)),
            dma((1,)),
            dma((1,)),
        ],
        compiler_params=pltpu.CompilerParams(
            collective_id=0, has_side_effects=True, vmem_limit_bytes=56 * 2**20
        ),
        name="scores_ring",
    )(queries.reshape(nb, rows_p, cols), train_grads, query_weight.reshape(1, rows_p))
    return scores, influence.reshape(n)


def solution(mesh):
    return jax.shard_map(
        functools.partial(body, mesh.shape["ex"], mesh.shape["proj"]),
        mesh=mesh,
        in_specs=(P("ex", "proj"), P("ex", "proj"), P("proj")),
        out_specs=(P("proj", "ex"), P("ex")),
        check_vma=False,
    )
```

time: 126 us -> 114 us (0.905)
  Pallas kernels: 122 us -> 110 us
    pallas_call x1, Pallas kernels: 122 us -> 110 us  [body(): pl.pallas_call(functools.partial(kernel, ex, proj), out_shape=(jax.ShapeD...]
where the time goes in v2:
time: 114 us; the launch traced here: 113 us
  Pallas kernels  110 us (96%)
  local copies, waits for them, and re-layouts  2.83 us (2%)
    pallas_call x1, Pallas kernels, body(): pl.pallas_call(functools.partial(kernel, ex, proj), out_shape=(jax.ShapeD...  110 us
    unnamed x2, local copies, waits for them, and re-layouts  2.83 us

profile of v2, /device:TPU:0, one launch (start us, length us, event | category | flops | bytes accessed | tf_op | source)
XLA Modules:
  0.0 113.1 jit_solution(8911724981556775177)
XLA Ops:
  0.6 109.6 %scores_ring.1 = (bf16[128,512]{1,0:T(8,128)(2,1)}, f32[1,512]{1,0:T(1,128)}) custom-call(bf16[2,128,8192]{2,1,0:T(8,128)(2,1)} %bitcast.3, bf16[512,8192]{1,0:T(8,128)(2,1)} %t_hbm.1, f32[1,128]{1,0:T(1,128)} %bitcast.5), custom_call_target="tpu_custom_call" | custom-call | tf_op jit(solution)/shard_map/scores_ring/pallas_call | solution.py:273
  110.3 1.6 %copy.7 = bf16[128,512]{1,0:T(8,128)(2,1)} copy(bf16[128,512]{1,0:T(8,128)(2,1)} %get-tuple-element.8) | data formatting | bytes 262144
  111.8 1.3 %copy.8 = f32[512]{0:T(512)} copy(f32[512]{0:T(512)} %bitcast.4) | data formatting | bytes 4096

commit v3 on v2

--- a/solution.py
+++ b/solution.py
@@ -11,6 +11,7 @@
 SLAB = 16
 FIRST = 2
 LANES = 128
+DEPTH = 2048
 PROMPT = 3
 
 
@@ -27,6 +28,8 @@
     chips = ex // 2
     half = proj // 2
     chunks = rows_p // SLAB
+    depth = min(cols, DEPTH)
+    pieces = cols // depth
     group = 2 * nb
     e = lax.axis_index("ex")
     p = lax.axis_index("proj")
@@ -52,23 +55,24 @@
 
     def send_y(i):
         d, c = i // chunks, lax.rem(i, chunks)
-        pltpu.make_async_remote_copy(
-            src_ref=q_hbm.at[:, rows_of(c)],
-            dst_ref=qbuf.at[pl.ds(e * nb, nb), rows_of(c)],
-            send_sem=y_send.at[d],
-            recv_sem=y_recv.at[d, c],
-            device_id={"ex": lax.rem(y + d + 1, chips) * 2 + core},
-            device_id_type=MESH,
-        ).start()
-
-    def sib_copy(s, c, own):
+        for j in range(pieces):
+            pltpu.make_async_remote_copy(
+                src_ref=q_hbm.at[:, rows_of(c), pl.ds(j * depth, depth)],
+                dst_ref=qbuf.at[pl.ds(e * nb, nb), rows_of(c), pl.ds(j * depth, depth)],
+                send_sem=y_send.at[d],
+                recv_sem=y_recv.at[d, c, j],
+                device_id={"ex": lax.rem(y + d + 1, chips) * 2 + core},
+                device_id_type=MESH,
+            ).start()
+
+    def sib_copy(s, c, j, own):
         at = (lax.rem(y - s + chips, chips) * 2 + core) * nb
-        dst = qbuf.at[pl.ds(at, nb), rows_of(c)]
+        dst = qbuf.at[pl.ds(at, nb), rows_of(c), pl.ds(j * depth, depth)]
         return pltpu.make_async_remote_copy(
-            src_ref=q_hbm.at[:, rows_of(c)] if own else dst,
+            src_ref=q_hbm.at[:, rows_of(c), pl.ds(j * depth, depth)] if own else dst,
             dst_ref=dst,
             send_sem=sib_send.at[s],
-            recv_sem=sib_recv.at[s, c],
+            recv_sem=sib_recv.at[s, c, j],
             device_id={"ex": sibling},
             device_id_type=MESH,
         )
@@ -94,7 +98,8 @@
     w_buf[0] = jnp.broadcast_to(w_ref[...], (8, rows_p))
     to_all(w_buf.at[0], lambda d: w_buf.at[d], w_send, w_recv)
     for c in range(chunks):
-        sib_copy(0, c, True).start()
+        for j in range(pieces):
+            sib_copy(0, c, j, True).start()
 
     def norms(count, at, load):
         def one(g, carry):
@@ -191,21 +196,26 @@
                 for k in range(2):
                     columns(lax.rem(y + d, chips) * 2 + k)
 
-        @pl.when(s > 0)
-        def _():
-            got = qbuf.at[pl.ds((chip * 2 + core) * nb, nb), rows_of(c)]
-            wait_for(got, y_recv.at[s - 1, c])
-            sib_copy(s, c, False).start()
-
-        wait_for(qbuf.at[pl.ds((chip * 2 + 1 - core) * nb, nb), rows_of(c)], sib_recv.at[s, c])
+        def take(j):
+            @pl.when(s > 0)
+            def _():
+                got = qbuf.at[pl.ds((chip * 2 + core) * nb, nb), rows_of(c), pl.ds(j * depth, depth)]
+                wait_for(got, y_recv.at[s - 1, c, j])
+                sib_copy(s, c, j, False).start()
+
         blocks = pl.ds(chip * group, group)
         pairs = pl.ds(chip * nb, nb)
-        depth = min(cols, 2048)
+        others = pl.ds((chip * 2 + 1 - core) * nb, nb)
         acc = jnp.zeros((group * SLAB, n), jnp.float32)
-        for k in range(0, cols, depth):
-            q = qbuf[blocks, rows_of(c), k : k + depth].reshape(group * SLAB, depth)
+        take(0)
+        for j in range(pieces):
+            if j + 1 < pieces:
+                take(j + 1)
+            at = pl.ds(j * depth, depth)
+            wait_for(qbuf.at[others, rows_of(c), at], sib_recv.at[s, c, j])
+            q = qbuf[blocks, rows_of(c), at].reshape(group * SLAB, depth)
             acc = acc + lax.dot_general(
-                q, tbuf[:, k : k + depth], (((1,), (1,)), ((), ())), preferred_element_type=jnp.float32
+                q, tbuf[:, at], (((1,), (1,)), ((), ())), preferred_element_type=jnp.float32
             )
         part[pairs, :, rows_of(c), :] = acc.reshape(nb, 2, SLAB, n)
         pltpu.make_async_remote_copy(
@@ -257,6 +267,11 @@
     wait_for(w_buf.at[pl.ds(1, proj - 1)], w_send.at[0])
     wait_for(q_rows.at[pl.ds(1, ex - 1)], n_send.at[0])
     wait_for(v_buf, v_send.at[0])
+
+
+def settle(scores_ref, infl_ref, scores_out, infl_out):
+    scores_out[...] = scores_ref[...]
+    infl_out[...] = infl_ref[0, :]
 
 
 def body(ex, proj, queries, train_grads, query_weight):
@@ -293,9 +308,9 @@
             pltpu.VMEM((proj - 1, 8, n), f32),
             dma((2,)),
             dma((chips - 1,)),
-            dma((chips - 1, chunks)),
+            dma((chips - 1, chunks, max(cols // DEPTH, 1))),
             dma((chips,)),
-            dma((chips, chunks)),
+            dma((chips, chunks, max(cols // DEPTH, 1))),
             dma((chips,)),
             dma((chips, chunks)),
             dma((1,)),
@@ -314,7 +329,13 @@
         ),
         name="scores_ring",
     )(queries.reshape(nb, rows_p, cols), train_grads, query_weight.reshape(1, rows_p))
-    return scores, influence.reshape(n)
+    return pl.pallas_call(
+        settle,
+        out_shape=(jax.ShapeDtypeStruct((rows_p, n), bf16), jax.ShapeDtypeStruct((n,), f32)),
+        in_specs=[vmem, vmem],
+        out_specs=(vmem, vmem),
+        name="settle",
+    )(scores, influence)
 
 
 def solution(mesh):

time: 114 us -> 111 us (0.974)
  local copies, waits for them, and re-layouts: 2.83 us -> 0 us
    unnamed x2 -> x0, local copies, waits for them, and re-layouts: 2.83 us -> none
    pallas_call x0 -> x1, Pallas kernels: none -> 1.57 us  [body(): pl.pallas_call(settle, out_shape=(jax.ShapeDtypeStruct((rows_p, n), bf16)...]
where the time goes in v3:
time: 111 us
  Pallas kernels  110 us (99%)
    pallas_call x1, Pallas kernels, body(): pl.pallas_call(functools.partial(kernel, ex, proj), out_shape=(jax.ShapeD...  109 us

profile of v3, /device:TPU:0, one launch (start us, length us, event | category | flops | bytes accessed | tf_op | source)
XLA Modules:
  0.0 111.1 jit_solution(6985249409159428646)
XLA Ops:
  0.6 108.8 %scores_ring.1 = (bf16[128,512]{1,0:T(8,128)(2,1)}, f32[1,512]{1,0:T(1,128)}) custom-call(bf16[2,128,8192]{2,1,0:T(8,128)(2,1)} %bitcast.2, bf16[512,8192]{1,0:T(8,128)(2,1)} %t_hbm.1, f32[1,128]{1,0:T(1,128)} %bitcast.3), custom_call_target="tpu_custom_call" | custom-call | tf_op jit(solution)/shard_map/scores_ring/pallas_call | solution.py:288
  109.5 1.6 %settle.1 = (bf16[128,512]{1,0:T(8,128)(2,1)}, f32[512]{0:T(512)}) custom-call(bf16[128,512]{1,0:T(8,128)(2,1)} %get-tuple-element.4.scores_ref, f32[1,512]{1,0:T(1,128)} %get-tuple-element.5.infl_ref), custom_call_target="tpu_custom_call" | custom-call | tf_op jit(solution)/shard_map/settle/pallas_call | solution.py:332

commit v4 on v3

--- a/solution.py
+++ b/solution.py
@@ -18,7 +18,7 @@
 def kernel(
     ex, proj, q_hbm, t_hbm, w_ref,
     scores_ref, infl_ref,
-    qbuf, tbuf, part, pair_buf, rs_buf, lanes, m_own, m_buf, w_buf, q_rows, q_col, wq_col, t_scale, v_own, v_buf,
+    qbuf, tbuf, part, pair_buf, rs_buf, lanes, m_own, m_buf, w_buf, q_rows, q_col, wq_col, t_scale, v_own, v_row, v_buf,
     load_sem, y_send, y_recv, sib_send, sib_recv, pair_send, pair_recv, rs_send, rs_recv,
     m_send, m_recv, w_send, w_recv, n_send, n_recv, v_send, v_recv,
 ):
@@ -231,7 +231,8 @@
 
         @pl.when(i == chips * chunks - 1)
         def _():
-            to_all(v_own, lambda d: v_buf.at[d - 1], v_send, v_recv)
+            v_row[...] = jnp.sum(v_own[...], axis=0, keepdims=True)
+            to_all(v_row, lambda d: v_buf.at[d - 1], v_send, v_recv)
 
         @pl.when((i > 0) & (i <= prompt))
         def _():
@@ -249,10 +250,10 @@
 
     lax.fori_loop(0, chips * chunks, step, 0)
     wait_for(v_buf, v_recv.at[0])
-    tot = v_own[...]
+    tot = v_row[...]
     for j in range(proj - 1):
         tot = tot + v_buf[j]
-    tot = jnp.sum(tot, axis=0, keepdims=True) * t_scale[0:1, :]
+    tot = tot * t_scale[0:1, :]
     infl_ref[...] = tot * (float(cols * proj) ** 0.5 * (proj * rows_p) ** (-0.5))
     for c in range(max(chunks - 2, 0), chunks):
         finish(jnp.int32(c))
@@ -305,7 +306,8 @@
             pltpu.VMEM((proj, rows_p, LANES), f32),
             pltpu.VMEM((8, n), f32),
             pltpu.VMEM((8, n), f32),
-            pltpu.VMEM((proj - 1, 8, n), f32),
+            pltpu.VMEM((1, n), f32),
+            pltpu.VMEM((proj - 1, 1, n), f32),
             dma((2,)),
             dma((chips - 1,)),
             dma((chips - 1, chunks, max(cols // DEPTH, 1))),

time: 111 us -> 110 us (level)
  no operation moved by 1% of the time
where the time goes in v4:
time: 110 us
  Pallas kernels  109 us (99%)
    pallas_call x1, Pallas kernels, body(): pl.pallas_call(functools.partial(kernel, ex, proj), out_shape=(jax.ShapeD...  108 us

profile of v4, /device:TPU:0, one launch (start us, length us, event | category | flops | bytes accessed | tf_op | source)
XLA Modules:
  0.0 110.1 jit_solution(4772970212955331870)
XLA Ops:
  0.6 107.9 %scores_ring.1 = (bf16[128,512]{1,0:T(8,128)(2,1)}, f32[1,512]{1,0:T(1,128)}) custom-call(bf16[2,128,8192]{2,1,0:T(8,128)(2,1)} %bitcast.2, bf16[512,8192]{1,0:T(8,128)(2,1)} %t_hbm.1, f32[1,128]{1,0:T(1,128)} %bitcast.3), custom_call_target="tpu_custom_call" | custom-call | tf_op jit(solution)/shard_map/scores_ring/pallas_call | solution.py:289
  108.6 1.6 %settle.1 = (bf16[128,512]{1,0:T(8,128)(2,1)}, f32[512]{0:T(512)}) custom-call(bf16[128,512]{1,0:T(8,128)(2,1)} %get-tuple-element.4.scores_ref, f32[1,512]{1,0:T(1,128)} %get-tuple-element.5.infl_ref), custom_call_target="tpu_custom_call" | custom-call | tf_op jit(solution)/shard_map/settle/pallas_call | solution.py:334
